TPU v7x, 32 devices: a whole 2x2x4 slice. The times are simulated.
32 devices in a mesh: grp: 2 (over x), gx: 16 (over z, y, core).
Axes of the slice: x: 2, y: 2, z: 4, core: 2. Of those that a mesh axis runs over, the one named last changes fastest.
Arguments:
- direction: float32 [64, 128, 128], P(('grp', 'gx')), parts along dimension 0, may hold values from -6 to 6
- kappa: float32 [64, 128, 128], P(('grp', 'gx')), parts along dimension 0, may hold values from 0.02 to 0.1
- velocity: float32 [3, 64, 128, 128], P(None, ('grp', 'gx')), parts along dimension 1, may hold values from -1 to 1
- prior_coef: float32 [64, 128, 128], P(('grp', 'gx')), parts along dimension 0, may hold values from 0.5 to 4
- noise_weight: float32 [4, 4096], P(None, ('grp', 'gx')), parts along dimension 1, may hold values from 1 to 10
- sensor_cell: int32 [4096], P(('grp', 'gx')), parts along dimension 0, may hold values from 0 to 32767
- sensor_slab: int32 [4096], P(('grp', 'gx')), parts along dimension 0, may hold values from 0 to 15
Outputs:
- hessian_action: float32 [64, 128, 128], P(('grp', 'gx')), parts along dimension 0
There are 2 independent parts, one for each index of `grp`. A program takes and returns all parts, laid end to end along the dimension named above; each array names one. Nothing has to cross between parts.
All inputs are finite; a program needn't handle non-finite values.
Results may differ from a plain program's by a relative error of at most 0.00002.
Values sent between devices are 32-bit elements; how exact they have to be, the bound alone decides.
A program may use at most 64 MiB of HBM per device.

v0:
```python
from functools import reduce

import jax
import jax.numpy as jnp
from jax import lax
from jax.sharding import PartitionSpec as P

STEPS = 4


time_step = 0.25
prior_scale = 0.01


def extended_2(block, sides, width):
    for axis, dim in sides:
        count = lax.axis_size(axis)
        forward = [(i, i + 1) for i in range(count - 1)]
        backward = [(target, source) for source, target in forward]
        low = lax.ppermute(
            lax.slice_in_dim(block, block.shape[dim] - width, None, axis=dim), axis, forward
        )
        high = lax.ppermute(lax.slice_in_dim(block, 0, width, axis=dim), axis, backward)
        block = jnp.concatenate([low, block, high], axis=dim)
    return block


def rate_terms(rates):
    kappa = rates[0]
    pieces = []
    for column in range(3):
        speed = rates[1 + column]
        pieces.append(time_step * (kappa + jax.nn.relu(-speed)))
        pieces.append(time_step * (kappa + jax.nn.relu(speed)))
    centre = 1.0 - reduce(lambda left, right: left + right, pieces)
    return [centre] + pieces


def cut_rows(term, start, offset, count):
    return term[start + offset : start + offset + count]


def forward_apply(extended, terms, start):
    count = extended.shape[0] - 2
    region = extended[1 : count + 1]
    padded = jnp.pad(region, ((0, 0), (1, 1), (1, 1)))
    sides = [cut_rows(term, start, 1, count) for term in terms]
    result = sides[0] * region + sides[1] * extended[2:] + sides[2] * extended[:count]
    result = result + sides[3] * padded[:, 2:, 1:-1] + sides[4] * padded[:, :-2, 1:-1]
    return result + sides[5] * padded[:, 1:-1, 2:] + sides[6] * padded[:, 1:-1, :-2]


def adjoint_apply(extended, terms, start):
    count = extended.shape[0] - 2
    region = extended[1 : count + 1]
    result = cut_rows(terms[0], start, 1, count) * region
    result = result + cut_rows(terms[1], start, 0, count) * extended[:count]
    result = result + cut_rows(terms[2], start, 2, count) * extended[2:]
    widths = ((0, 0), (1, 1), (1, 1))
    up_y = jnp.pad(cut_rows(terms[3], start, 1, count) * region, widths)
    down_y = jnp.pad(cut_rows(terms[4], start, 1, count) * region, widths)
    up_z = jnp.pad(cut_rows(terms[5], start, 1, count) * region, widths)
    down_z = jnp.pad(cut_rows(terms[6], start, 1, count) * region, widths)
    result = result + up_y[:, :-2, 1:-1] + down_y[:, 2:, 1:-1]
    return result + up_z[:, 1:-1, :-2] + down_z[:, 1:-1, 2:]


def prior_apply(extended, coef_wide, start):
    count = extended.shape[0] - 2
    region = extended[1 : count + 1]
    padded = jnp.pad(region, ((0, 0), (1, 1), (1, 1)))
    result = (cut_rows(coef_wide, start, 1, count) + 6.0) * region - extended[2:] - extended[:count]
    result = result - padded[:, 2:, 1:-1] - padded[:, :-2, 1:-1]
    return result - padded[:, 1:-1, 2:] - padded[:, 1:-1, :-2]


def on_device(direction, kappa, velocity, prior_coef, noise_weight, sensor_cell, sensor_slab):
    slab_x, cols_y, cols_z = direction.shape
    plane = cols_y * cols_z
    position = lax.axis_index("gx")
    width = 1
    rates = jnp.concatenate([kappa[None], velocity, prior_coef[None]], 0)
    wide_rates = extended_2(rates, (("gx", 1),), width)
    terms = rate_terms(wide_rates[:4])
    prior_wide = wide_rates[4]
    cells, slabs = (
        lax.all_gather(sensor_cell, "gx", axis=0, tiled=True),
        lax.all_gather(sensor_slab, "gx", axis=0, tiled=True),
    )
    mine = slabs == position
    anchor = position * slab_x
    sensor_x = slabs * slab_x + cells // plane
    sensor_rest = cells % plane
    weighted_rows = []

    def record(state, step):
        values = jnp.where(mine, jnp.take(state.reshape(-1), cells), 0.0)
        owned = lax.psum_scatter(values, "gx", scatter_dimension=0, tiled=True)
        weighted_rows.append(noise_weight[step] * owned)

    state = direction
    for step in range(STEPS):
        extended = extended_2(state, (("gx", 0),), 1)
        state = forward_apply(extended, terms, 0)
        record(state, step)
    adjoint_field = jnp.zeros_like(direction)
    for step in reversed(range(STEPS)):
        add_misfit = lax.all_gather(weighted_rows[step], "gx", axis=0, tiled=True)
        length = adjoint_field.shape[0]
        relative = sensor_x - anchor
        valid = (relative >= 0) & (relative < length)
        target = jnp.where(valid, relative * plane + sensor_rest, 0)
        flat_field = adjoint_field.reshape(-1).at[target].add(jnp.where(valid, add_misfit, 0.0))
        adjoint_field = flat_field.reshape(adjoint_field.shape)
        extended = extended_2(adjoint_field, (("gx", 0),), 1)
        adjoint_field = adjoint_apply(extended, terms, 0)
    extended = extended_2(direction, (("gx", 0),), 1)
    halfway = prior_apply(extended, prior_wide, 0)
    extended = extended_2(halfway, (("gx", 0),), 1)
    smooth = prior_apply(extended, prior_wide, 0)
    return adjoint_field + prior_scale * smooth


def solution(mesh):
    return jax.shard_map(
        on_device,
        mesh=mesh,
        in_specs=(
            P(("grp", "gx"), None, None),
            P(("grp", "gx"), None, None),
            P(None, ("grp", "gx"), None, None),
            P(("grp", "gx"), None, None),
            P(None, ("grp", "gx")),
            P(("grp", "gx")),
            P(("grp", "gx")),
        ),
        out_specs=P(("grp", "gx"), None, None),
        check_vma=False,
    )
```

profile of v0, /device:TPU:5, one launch (start us, length us, event | category | flops | bytes accessed | tf_op | source)
XLA Modules:
  0.0 344.8 jit_solution(9943111720859592520)
XLA Ops:
  0.0 1.1 pad_maximum_fusion
  1.1 0.0 copy-start.3
  1.2 0.0 copy-start
  1.2 3.8 %collective-permute-start = (f32[5,1,128,128]{3,2,1,0:T(8,128)S(1)}, f32[5,1,128,128]{3,2,1,0:T(8,128)S(1)}, u32[]{:S(2)}, u32[]{:S(2)}) collective-permute-start(f32[5,1,128,128]{3,2,1,0:T(8,128)S(1)} %get-tuple-element.26), channel_id=1, source_target_pairs={{0,1},{1,2},{2,3},{3,4},{4,5},{5,6},{6,7},{7,8},{8,9},{9,10},{10,1... | collective-permute-start | bytes 983048 | tf_op jit(solution)/shard_map/ppermute | solution.py:20
  5.1 0.0 copy-start.1
  5.1 0.0 copy-start.2
  5.1 2.1 collective-permute-start.1
  7.2 2.5 collective-permute-start.2
  9.7 0.0 copy-start.5
  9.7 3.9 %collective-permute-start.3 = (f32[1,128,128]{2,1,0:T(8,128)S(1)}, f32[1,128,128]{2,1,0:T(8,128)S(1)}, u32[]{:S(2)}, u32[]{:S(2)}) collective-permute-start(f32[1,128,128]{2,1,0:T(8,128)S(1)} %get-tuple-element.64), channel_id=1, source_target_pairs={{0,1},{1,2},{2,3},{3,4},{4,5},{5,6},{6,7},{7,8},{8,9},{9,10},{10,1... | collective-permute-start | bytes 196616 | tf_op jit(solution)/shard_map/ppermute | solution.py:20
  13.7 17.0 %all-gather.1 = s32[16,1,128]{2,1,0:T(1,128)S(1)} all-gather(s32[1,1,128]{2,1,0:T(1,128)S(1)} %bitcast.213), channel_id=1, replica_groups=mesh['grp'=2,'gx'=16] {'gx'}, dimensions={0}, use_global_device_ids=true | all-gather | bytes 8704 | tf_op jit(solution)/shard_map/all_gather | solution.py:87
  30.7 0.7 copy-done.6
  31.3 20.3 %all-gather = s32[16,1,128]{2,1,0:T(1,128)S(1)} all-gather(s32[1,1,128]{2,1,0:T(1,128)S(1)} %bitcast.214), channel_id=1, replica_groups=mesh['grp'=2,'gx'=16] {'gx'}, dimensions={0}, use_global_device_ids=true | all-gather | bytes 8704 | tf_op jit(solution)/shard_map/all_gather | solution.py:88
  51.7 0.1 add_multiply_fusion.3
  51.7 0.1 add_multiply_fusion.1
  51.9 0.1 add_multiply_fusion
  52.0 0.0 collective-permute-done.2
  52.0 0.2 fusion.76
  52.2 2.1 collective-permute-start.4
  54.3 4.4 %collective-permute-start.5 = (f32[1,128,128]{2,1,0:T(8,128)S(1)}, f32[1,128,128]{2,1,0:T(8,128)S(1)}, u32[]{:S(2)}, u32[]{:S(2)}) collective-permute-start(f32[1,128,128]{2,1,0:T(8,128)S(1)} %get-tuple-element.63), channel_id=1, source_target_pairs={{0,1},{1,2},{2,3},{3,4},{4,5},{5,6},{6,7},{7,8},{8,9},{9,10},{10,1... | collective-permute-start | bytes 196616 | tf_op jit(solution)/shard_map/ppermute | solution.py:20
  58.7 0.0 copy-start.7
  58.7 0.6 copy-done.7
  59.4 0.6 dynamic-slice
  60.6 0.0 collective-permute-done.5
  60.6 0.1 fusion.21
  60.8 1.9 collective-permute-start.6
  62.7 4.5 %collective-permute-start.7 = (f32[1,128,128]{2,1,0:T(8,128)S(1)}, f32[1,128,128]{2,1,0:T(8,128)S(1)}, u32[]{:S(2)}, u32[]{:S(2)}) collective-permute-start(f32[1,128,128]{2,1,0:T(8,128)S(1)} %get-tuple-element.61), channel_id=1, source_target_pairs={{0,1},{1,2},{2,3},{3,4},{4,5},{5,6},{6,7},{7,8},{8,9},{9,10},{10,1... | collective-permute-start | bytes 196616 | tf_op jit(solution)/shard_map/ppermute | solution.py:20
  67.3 1.9 collective-permute-start.18
  69.2 4.5 %collective-permute-start.19 = (f32[1,128,128]{2,1,0:T(8,128)S(1)}, f32[1,128,128]{2,1,0:T(8,128)S(1)}, u32[]{:S(2)}, u32[]{:S(2)}) collective-permute-start(f32[1,128,128]{2,1,0:T(8,128)S(1)} %get-tuple-element.35), channel_id=1, source_target_pairs={{0,1},{1,2},{2,3},{3,4},{4,5},{5,6},{6,7},{7,8},{8,9},{9,10},{10,1... | collective-permute-start | bytes 196616 | tf_op jit(solution)/shard_map/ppermute | solution.py:20
  73.8 11.8 %gather_fusion.3 = f32[2048]{0:T(1024)S(1)} fusion(f32[32768]{0:T(1024)S(1)} %bitcast.190, s32[2048]{0:T(1024)S(1)} %fusion.89), kind=kCustom, calls=%fused_computation.3.clone | custom fusion | bytes 24576 | tf_op jit(solution)/shard_map/jit(_take)/gather | solution.py:97
  85.6 0.1 fusion.29
  85.8 1.9 collective-permute-start.8
  87.7 4.5 %collective-permute-start.9 = (f32[1,128,128]{2,1,0:T(8,128)S(1)}, f32[1,128,128]{2,1,0:T(8,128)S(1)}, u32[]{:S(2)}, u32[]{:S(2)}) collective-permute-start(f32[1,128,128]{2,1,0:T(8,128)S(1)} %get-tuple-element.59), channel_id=1, source_target_pairs={{0,1},{1,2},{2,3},{3,4},{4,5},{5,6},{6,7},{7,8},{8,9},{9,10},{10,1... | collective-permute-start | bytes 196616 | tf_op jit(solution)/shard_map/ppermute | solution.py:20
  92.2 11.8 %gather_fusion.2 = f32[2048]{0:T(1024)S(1)} fusion(f32[32768]{0:T(1024)S(1)} %bitcast.191, s32[2048]{0:T(1024)S(1)} %fusion.89), kind=kCustom, calls=%fused_computation.2.clone | custom fusion | bytes 24576 | tf_op jit(solution)/shard_map/jit(_take)/gather | solution.py:97
  104.0 11.8 %gather_fusion.1 = f32[2048]{0:T(1024)S(1)} fusion(f32[32768]{0:T(1024)S(1)} %bitcast.192, s32[2048]{0:T(1024)S(1)} %fusion.89), kind=kCustom, calls=%fused_computation.1.clone | custom fusion | bytes 24576 | tf_op jit(solution)/shard_map/jit(_take)/gather | solution.py:97
  115.8 0.1 fusion.37
  116.0 11.8 %gather_fusion = f32[2048]{0:T(1024)S(1)} fusion(f32[32768]{0:T(1024)S(1)} %bitcast.193, s32[2048]{0:T(1024)S(1)} %fusion.89), kind=kCustom, calls=%fused_computation.clone | custom fusion | bytes 24576 | tf_op jit(solution)/shard_map/jit(_take)/gather | solution.py:97
  127.8 45.4 %all-reduce.25 = (f32[2048]{0:T(1024)S(1)}, f32[2048]{0:T(1024)S(1)}, f32[2048]{0:T(1024)S(1)}, f32[2048]{0:T(1024)S(1)}) all-reduce(f32[2048]{0:T(1024)S(1)} %get-tuple-element.68, f32[2048]{0:T(1024)S(1)} %get-tuple-element.67, f32[2048]{0:T(1024)S(1)} %get-tuple-element.66, ...), channel_id=2, replica_groups=mesh['grp'=2,'gx'=16] {'gx'}, use_global_device_ids=true, to_apply=%region_0.2.clone | all-reduce | flops 8192 | bytes 65536
  173.2 0.7 copy-done.4
  173.9 0.1 fusion.92
  174.0 26.7 %all-gather.5 = f32[16,1,128]{2,1,0:T(1,128)S(1)} all-gather(f32[1,1,128]{2,1,0:T(1,128)S(1)} %get-tuple-element.73), channel_id=1, replica_groups=mesh['grp'=2,'gx'=16] {'gx'}, dimensions={0}, use_global_device_ids=true | all-gather | bytes 8704 | tf_op jit(solution)/shard_map/all_gather | solution.py:108
  200.7 17.0 %all-gather.2 = f32[16,1,128]{2,1,0:T(1,128)S(1)} all-gather(f32[1,1,128]{2,1,0:T(1,128)S(1)} %get-tuple-element.75), channel_id=1, replica_groups=mesh['grp'=2,'gx'=16] {'gx'}, dimensions={0}, use_global_device_ids=true | all-gather | bytes 8704 | tf_op jit(solution)/shard_map/all_gather | solution.py:108
  217.7 19.0 %all-gather.3 = f32[16,1,128]{2,1,0:T(1,128)S(1)} all-gather(f32[1,1,128]{2,1,0:T(1,128)S(1)} %get-tuple-element.74), channel_id=1, replica_groups=mesh['grp'=2,'gx'=16] {'gx'}, dimensions={0}, use_global_device_ids=true | all-gather | bytes 8704 | tf_op jit(solution)/shard_map/all_gather | solution.py:108
  236.7 17.3 %all-gather.4 = f32[16,1,128]{2,1,0:T(1,128)S(1)} all-gather(f32[1,1,128]{2,1,0:T(1,128)S(1)} %get-tuple-element.72), channel_id=1, replica_groups=mesh['grp'=2,'gx'=16] {'gx'}, dimensions={0}, use_global_device_ids=true | all-gather | bytes 8704 | tf_op jit(solution)/shard_map/all_gather | solution.py:108
  254.0 13.9 %scatter_custom_fusion = f32[32768]{0:T(1024)S(1)} fusion(s32[2048]{0:T(1024)S(1)} %compare_select_fusion, f32[2048]{0:T(1024)S(1)} %get-tuple-element.71, f32[]{:T(128)} %constant.56.clone.1), kind=kCustom, calls=%fused_computation.200 | custom fusion | flops 2048 | bytes 131076 | tf_op jit(solution)/shard_map/scatter-add | solution.py:113
  267.9 1.9 collective-permute-start.10
  269.8 2.4 collective-permute-start.11
  272.3 4.0 %collective-permute-done.11 = f32[1,128,128]{2,1,0:T(8,128)S(1)} collective-permute-done((f32[1,128,128]{2,1,0:T(8,128)S(1)}, f32[1,128,128]{2,1,0:T(8,128)S(1)}, u32[]{:S(2)}, u32[]{:S(2)}) %collective-permute-start.11) | collective-permute-done | bytes 65568 | tf_op jit(solution)/shard_map/ppermute | solution.py:23
  276.3 0.2 fusion.3
  276.5 13.9 %scatter_fusion = f32[32768]{0:T(1024)S(1)} fusion(f32[32768]{0:T(1024)S(1)} %bitcast.187, s32[2048]{0:T(1024)S(1)} %compare_select_fusion, f32[2048]{0:T(1024)S(1)} %get-tuple-element.70), kind=kCustom, calls=%fused_computation.5 | custom fusion | flops 2048 | bytes 32768 | tf_op jit(solution)/shard_map/scatter-add | solution.py:113
  290.4 1.9 collective-permute-start.12
  292.4 2.4 collective-permute-start.13
  294.8 4.0 %collective-permute-done.13 = f32[1,128,128]{2,1,0:T(8,128)S(1)} collective-permute-done((f32[1,128,128]{2,1,0:T(8,128)S(1)}, f32[1,128,128]{2,1,0:T(8,128)S(1)}, u32[]{:S(2)}, u32[]{:S(2)}) %collective-permute-start.13) | collective-permute-done | bytes 65568 | tf_op jit(solution)/shard_map/ppermute | solution.py:23
  298.9 0.2 fusion.7
  299.0 13.9 %scatter_fusion.1 = f32[32768]{0:T(1024)S(1)} fusion(f32[32768]{0:T(1024)S(1)} %bitcast.184, s32[2048]{0:T(1024)S(1)} %compare_select_fusion, f32[2048]{0:T(1024)S(1)} %get-tuple-element.69), kind=kCustom, calls=%fused_computation.6 | custom fusion | flops 2048 | bytes 32768 | tf_op jit(solution)/shard_map/scatter-add | solution.py:113
  313.0 1.9 collective-permute-start.14
  314.9 2.4 collective-permute-start.15
  317.4 4.0 %collective-permute-done.15 = f32[1,128,128]{2,1,0:T(8,128)S(1)} collective-permute-done((f32[1,128,128]{2,1,0:T(8,128)S(1)}, f32[1,128,128]{2,1,0:T(8,128)S(1)}, u32[]{:S(2)}, u32[]{:S(2)}) %collective-permute-start.15) | collective-permute-done | bytes 65568 | tf_op jit(solution)/shard_map/ppermute | solution.py:23
  321.4 0.2 fusion.11
  321.6 13.9 %scatter_fusion.2 = f32[32768]{0:T(1024)S(1)} fusion(f32[32768]{0:T(1024)S(1)} %bitcast.181, s32[2048]{0:T(1024)S(1)} %compare_select_fusion, f32[2048]{0:T(1024)S(1)} %get-tuple-element.10), kind=kCustom, calls=%fused_computation.7 | custom fusion | flops 2048 | bytes 32768 | tf_op jit(solution)/shard_map/scatter-add | solution.py:113
  335.5 1.9 collective-permute-start.16
  337.5 2.4 collective-permute-start.17
  339.9 4.0 %collective-permute-done.17 = f32[1,128,128]{2,1,0:T(8,128)S(1)} collective-permute-done((f32[1,128,128]{2,1,0:T(8,128)S(1)}, f32[1,128,128]{2,1,0:T(8,128)S(1)}, u32[]{:S(2)}, u32[]{:S(2)}) %collective-permute-start.17) | collective-permute-done | bytes 65568 | tf_op jit(solution)/shard_map/ppermute | solution.py:23
  343.9 0.9 fusion.16
  (42 shorter events, 0.4 us)
Async XLA Ops:
  1.1 6.0 %copy-start.3 = (f32[2,128,128]{2,1,0:T(8,128)S(1)}, f32[2,128,128]{2,1,0:T(8,128)}, u32[]{:S(2)}) copy-start(f32[2,128,128]{2,1,0:T(8,128)} %param.9) | copy-start | bytes 393220
  1.2 50.5 %copy-start = (f32[3,2,128,128]{3,2,1,0:T(8,128)S(1)}, f32[3,2,128,128]{3,2,1,0:T(8,128)}, u32[]{:S(2)}) copy-start(f32[3,2,128,128]{3,2,1,0:T(8,128)} %param.11) | copy-start | bytes 1179652
  1.2 50.4 %collective-permute-start = (f32[5,1,128,128]{3,2,1,0:T(8,128)S(1)}, f32[5,1,128,128]{3,2,1,0:T(8,128)S(1)}, u32[]{:S(2)}, u32[]{:S(2)}) collective-permute-start(f32[5,1,128,128]{3,2,1,0:T(8,128)S(1)} %get-tuple-element.26), channel_id=1, source_target_pairs={{0,1},{1,2},{2,3},{3,4},{4,5},{5,6},{6,7},{7,8},{8,9},{9,10},{10,1... | collective-permute-start | bytes 983048 | tf_op jit(solution)/shard_map/ppermute | solution.py:20
  5.1 46.6 %copy-start.1 = (f32[2,128,128]{2,1,0:T(8,128)S(1)}, f32[2,128,128]{2,1,0:T(8,128)}, u32[]{:S(2)}) copy-start(f32[2,128,128]{2,1,0:T(8,128)} %param.12) | copy-start | bytes 393220
  5.1 46.6 %copy-start.2 = (f32[2,128,128]{2,1,0:T(8,128)S(1)}, f32[2,128,128]{2,1,0:T(8,128)}, u32[]{:S(2)}) copy-start(f32[2,128,128]{2,1,0:T(8,128)} %param.10) | copy-start | bytes 393220
  5.1 46.5 %collective-permute-start.1 = (f32[5,1,128,128]{3,2,1,0:T(8,128)S(1)}, f32[5,1,128,128]{3,2,1,0:T(8,128)S(1)}, u32[]{:S(2)}, u32[]{:S(2)}) collective-permute-start(f32[5,1,128,128]{3,2,1,0:T(8,128)S(1)} %get-tuple-element.27), channel_id=1, source_target_pairs={{1,0},{2,1},{3,2},{4,3},{5,4},{6,5},{7,6},{8,7},{9,8},{10,9},{11,1... | collective-permute-start | bytes 983048 | tf_op jit(solution)/shard_map/ppermute | solution.py:23
  7.2 44.8 %collective-permute-start.2 = (f32[1,128,128]{2,1,0:T(8,128)S(1)}, f32[1,128,128]{2,1,0:T(8,128)S(1)}, u32[]{:S(2)}, u32[]{:S(2)}) collective-permute-start(f32[1,128,128]{2,1,0:T(8,128)S(1)} %get-tuple-element.65), channel_id=1, source_target_pairs={{1,0},{2,1},{3,2},{4,3},{5,4},{6,5},{7,6},{8,7},{9,8},{10,9},{11,1... | collective-permute-start | bytes 196616 | tf_op jit(solution)/shard_map/ppermute | solution.py:23
  9.7 4.0 %copy-start.5 = (s32[128]{0:T(128)S(1)}, s32[128]{0:T(128)}, u32[]{:S(2)}) copy-start(s32[128]{0:T(128)} %param.14) | copy-start | bytes 1540
  9.7 42.2 %collective-permute-start.3 = (f32[1,128,128]{2,1,0:T(8,128)S(1)}, f32[1,128,128]{2,1,0:T(8,128)S(1)}, u32[]{:S(2)}, u32[]{:S(2)}) collective-permute-start(f32[1,128,128]{2,1,0:T(8,128)S(1)} %get-tuple-element.64), channel_id=1, source_target_pairs={{0,1},{1,2},{2,3},{3,4},{4,5},{5,6},{6,7},{7,8},{8,9},{9,10},{10,1... | collective-permute-start | bytes 196616 | tf_op jit(solution)/shard_map/ppermute | solution.py:20
  30.7 0.7 copy-start.6
  52.2 8.4 %collective-permute-start.4 = (f32[1,128,128]{2,1,0:T(8,128)S(1)}, f32[1,128,128]{2,1,0:T(8,128)S(1)}, u32[]{:S(2)}, u32[]{:S(2)}) collective-permute-start(f32[1,128,128]{2,1,0:T(8,128)S(1)} %get-tuple-element.62), channel_id=1, source_target_pairs={{1,0},{2,1},{3,2},{4,3},{5,4},{6,5},{7,6},{8,7},{9,8},{10,9},{11,1... | collective-permute-start | bytes 196616 | tf_op jit(solution)/shard_map/ppermute | solution.py:23
  54.3 6.3 %collective-permute-start.5 = (f32[1,128,128]{2,1,0:T(8,128)S(1)}, f32[1,128,128]{2,1,0:T(8,128)S(1)}, u32[]{:S(2)}, u32[]{:S(2)}) collective-permute-start(f32[1,128,128]{2,1,0:T(8,128)S(1)} %get-tuple-element.63), channel_id=1, source_target_pairs={{0,1},{1,2},{2,3},{3,4},{4,5},{5,6},{6,7},{7,8},{8,9},{9,10},{10,1... | collective-permute-start | bytes 196616 | tf_op jit(solution)/shard_map/ppermute | solution.py:20
  58.7 0.7 copy-start.7
  60.8 24.8 %collective-permute-start.6 = (f32[1,128,128]{2,1,0:T(8,128)S(1)}, f32[1,128,128]{2,1,0:T(8,128)S(1)}, u32[]{:S(2)}, u32[]{:S(2)}) collective-permute-start(f32[1,128,128]{2,1,0:T(8,128)S(1)} %get-tuple-element.60), channel_id=1, source_target_pairs={{1,0},{2,1},{3,2},{4,3},{5,4},{6,5},{7,6},{8,7},{9,8},{10,9},{11,1... | collective-permute-start | bytes 196616 | tf_op jit(solution)/shard_map/ppermute | solution.py:23
  62.7 22.8 %collective-permute-start.7 = (f32[1,128,128]{2,1,0:T(8,128)S(1)}, f32[1,128,128]{2,1,0:T(8,128)S(1)}, u32[]{:S(2)}, u32[]{:S(2)}) collective-permute-start(f32[1,128,128]{2,1,0:T(8,128)S(1)} %get-tuple-element.61), channel_id=1, source_target_pairs={{0,1},{1,2},{2,3},{3,4},{4,5},{5,6},{6,7},{7,8},{8,9},{9,10},{10,1... | collective-permute-start | bytes 196616 | tf_op jit(solution)/shard_map/ppermute | solution.py:20
  67.3 272.6 %collective-permute-start.18 = (f32[1,128,128]{2,1,0:T(8,128)S(1)}, f32[1,128,128]{2,1,0:T(8,128)S(1)}, u32[]{:S(2)}, u32[]{:S(2)}) collective-permute-start(f32[1,128,128]{2,1,0:T(8,128)S(1)} %get-tuple-element.34), channel_id=1, source_target_pairs={{1,0},{2,1},{3,2},{4,3},{5,4},{6,5},{7,6},{8,7},{9,8},{10,9},{11,1... | collective-permute-start | bytes 196616 | tf_op jit(solution)/shard_map/ppermute | solution.py:23
  69.2 270.7 %collective-permute-start.19 = (f32[1,128,128]{2,1,0:T(8,128)S(1)}, f32[1,128,128]{2,1,0:T(8,128)S(1)}, u32[]{:S(2)}, u32[]{:S(2)}) collective-permute-start(f32[1,128,128]{2,1,0:T(8,128)S(1)} %get-tuple-element.35), channel_id=1, source_target_pairs={{0,1},{1,2},{2,3},{3,4},{4,5},{5,6},{6,7},{7,8},{8,9},{9,10},{10,1... | collective-permute-start | bytes 196616 | tf_op jit(solution)/shard_map/ppermute | solution.py:20
  85.8 30.1 %collective-permute-start.8 = (f32[1,128,128]{2,1,0:T(8,128)S(1)}, f32[1,128,128]{2,1,0:T(8,128)S(1)}, u32[]{:S(2)}, u32[]{:S(2)}) collective-permute-start(f32[1,128,128]{2,1,0:T(8,128)S(1)} %get-tuple-element.58), channel_id=1, source_target_pairs={{1,0},{2,1},{3,2},{4,3},{5,4},{6,5},{7,6},{8,7},{9,8},{10,9},{11,1... | collective-permute-start | bytes 196616 | tf_op jit(solution)/shard_map/ppermute | solution.py:23
  87.7 28.2 %collective-permute-start.9 = (f32[1,128,128]{2,1,0:T(8,128)S(1)}, f32[1,128,128]{2,1,0:T(8,128)S(1)}, u32[]{:S(2)}, u32[]{:S(2)}) collective-permute-start(f32[1,128,128]{2,1,0:T(8,128)S(1)} %get-tuple-element.59), channel_id=1, source_target_pairs={{0,1},{1,2},{2,3},{3,4},{4,5},{5,6},{6,7},{7,8},{8,9},{9,10},{10,1... | collective-permute-start | bytes 196616 | tf_op jit(solution)/shard_map/ppermute | solution.py:20
  173.2 0.7 copy-start.4
  267.9 4.4 %collective-permute-start.10 = (f32[1,128,128]{2,1,0:T(8,128)S(1)}, f32[1,128,128]{2,1,0:T(8,128)S(1)}, u32[]{:S(2)}, u32[]{:S(2)}) collective-permute-start(f32[1,128,128]{2,1,0:T(8,128)S(1)} %get-tuple-element.52), channel_id=1, source_target_pairs={{0,1},{1,2},{2,3},{3,4},{4,5},{5,6},{6,7},{7,8},{8,9},{9,10},{10,1... | collective-permute-start | bytes 196616 | tf_op jit(solution)/shard_map/ppermute | solution.py:20
  269.8 6.5 %collective-permute-start.11 = (f32[1,128,128]{2,1,0:T(8,128)S(1)}, f32[1,128,128]{2,1,0:T(8,128)S(1)}, u32[]{:S(2)}, u32[]{:S(2)}) collective-permute-start(f32[1,128,128]{2,1,0:T(8,128)S(1)} %get-tuple-element.53), channel_id=1, source_target_pairs={{1,0},{2,1},{3,2},{4,3},{5,4},{6,5},{7,6},{8,7},{9,8},{10,9},{11,1... | collective-permute-start | bytes 196616 | tf_op jit(solution)/shard_map/ppermute | solution.py:23
  290.4 4.4 %collective-permute-start.12 = (f32[1,128,128]{2,1,0:T(8,128)S(1)}, f32[1,128,128]{2,1,0:T(8,128)S(1)}, u32[]{:S(2)}, u32[]{:S(2)}) collective-permute-start(f32[1,128,128]{2,1,0:T(8,128)S(1)} %get-tuple-element.46), channel_id=1, source_target_pairs={{0,1},{1,2},{2,3},{3,4},{4,5},{5,6},{6,7},{7,8},{8,9},{9,10},{10,1... | collective-permute-start | bytes 196616 | tf_op jit(solution)/shard_map/ppermute | solution.py:20
  292.4 6.5 %collective-permute-start.13 = (f32[1,128,128]{2,1,0:T(8,128)S(1)}, f32[1,128,128]{2,1,0:T(8,128)S(1)}, u32[]{:S(2)}, u32[]{:S(2)}) collective-permute-start(f32[1,128,128]{2,1,0:T(8,128)S(1)} %get-tuple-element.47), channel_id=1, source_target_pairs={{1,0},{2,1},{3,2},{4,3},{5,4},{6,5},{7,6},{8,7},{9,8},{10,9},{11,1... | collective-permute-start | bytes 196616 | tf_op jit(solution)/shard_map/ppermute | solution.py:23
  313.0 4.4 %collective-permute-start.14 = (f32[1,128,128]{2,1,0:T(8,128)S(1)}, f32[1,128,128]{2,1,0:T(8,128)S(1)}, u32[]{:S(2)}, u32[]{:S(2)}) collective-permute-start(f32[1,128,128]{2,1,0:T(8,128)S(1)} %get-tuple-element.40), channel_id=1, source_target_pairs={{0,1},{1,2},{2,3},{3,4},{4,5},{5,6},{6,7},{7,8},{8,9},{9,10},{10,1... | collective-permute-start | bytes 196616 | tf_op jit(solution)/shard_map/ppermute | solution.py:20
  314.9 6.5 %collective-permute-start.15 = (f32[1,128,128]{2,1,0:T(8,128)S(1)}, f32[1,128,128]{2,1,0:T(8,128)S(1)}, u32[]{:S(2)}, u32[]{:S(2)}) collective-permute-start(f32[1,128,128]{2,1,0:T(8,128)S(1)} %get-tuple-element.41), channel_id=1, source_target_pairs={{1,0},{2,1},{3,2},{4,3},{5,4},{6,5},{7,6},{8,7},{9,8},{10,9},{11,1... | collective-permute-start | bytes 196616 | tf_op jit(solution)/shard_map/ppermute | solution.py:23
  335.5 4.4 %collective-permute-start.16 = (f32[1,128,128]{2,1,0:T(8,128)S(1)}, f32[1,128,128]{2,1,0:T(8,128)S(1)}, u32[]{:S(2)}, u32[]{:S(2)}) collective-permute-start(f32[1,128,128]{2,1,0:T(8,128)S(1)} %get-tuple-element.32), channel_id=1, source_target_pairs={{0,1},{1,2},{2,3},{3,4},{4,5},{5,6},{6,7},{7,8},{8,9},{9,10},{10,1... | collective-permute-start | bytes 196616 | tf_op jit(solution)/shard_map/ppermute | solution.py:20
  337.5 6.5 %collective-permute-start.17 = (f32[1,128,128]{2,1,0:T(8,128)S(1)}, f32[1,128,128]{2,1,0:T(8,128)S(1)}, u32[]{:S(2)}, u32[]{:S(2)}) collective-permute-start(f32[1,128,128]{2,1,0:T(8,128)S(1)} %get-tuple-element.33), channel_id=1, source_target_pairs={{1,0},{2,1},{3,2},{4,3},{5,4},{6,5},{7,6},{8,7},{9,8},{10,9},{11,1... | collective-permute-start | bytes 196616 | tf_op jit(solution)/shard_map/ppermute | solution.py:23
where the time goes:
time: 346 us; the launch traced here: 345 us
  blocking collectives  163 us (47%)
  other arithmetic  59.4 us (17%)
  starting transfers between devices  55.5 us (16%)
  local copies, waits for them, and re-layouts  49.9 us (14%)
  waiting for transfers between devices  16.1 us (5%)
    all_gather x4, blocking collectives, on_device(): add_misfit = lax.all_gather(weighted_rows[step], 'gx', axis=0, tiled=True)  80 us
    scatter-add x4, other arithmetic, on_device(): adjoint_field.reshape(-1).at[target].add(jnp.where(valid, add_misfit, 0.0))  55.7 us
    gather x4, local copies, waits for them, and re-layouts, record(): values = jnp.where(mine, jnp.take(state.reshape(-1), cells), 0.0)  47.1 us
    unnamed x1, blocking collectives  45.4 us
    ppermute x10, starting transfers between devices, extended_2(): lax.ppermute(lax.slice_in_dim(block, block.shape[dim] - width, None, axis...  33.5 us
    ppermute x10, starting transfers between devices, extended_2(): lax.ppermute(lax.slice_in_dim(block, 0, width, axis=dim), axis, backward)  22 us
    all_gather x1, blocking collectives, on_device(): lax.all_gather(sensor_slab, 'gx', axis=0, tiled=True)  20.3 us
    all_gather x1, blocking collectives, on_device(): lax.all_gather(sensor_cell, 'gx', axis=0, tiled=True)  17 us
  transfers between devices with their start and end apart: 20, of which 4 were waited for; matrix products, arithmetic and copies ran while one was open for 30% of the time, Pallas kernels for 0%

commit v1 on v0

v1 whole, which is shorter than its diff:
```python
import functools

import jax
import jax.numpy as jnp
from jax import lax
from jax.experimental import pallas as pl
from jax.experimental.pallas import tpu as pltpu
from jax.sharding import PartitionSpec as P

STEPS = 4
CHUNKS = 2
GROUP = 16

time_step = 0.25
prior_scale = 0.01


def kernel(
    count,
    direction_hbm,
    kappa_hbm,
    velocity_hbm,
    prior_hbm,
    noise_ref,
    cell_ref,
    slab_ref,
    out_hbm,
    states,
    kappa,
    velocity,
    prior,
    centre,
    coef,
    pre,
    smooth,
    half,
    sends,
    halo_low,
    halo_high,
    tiles,
    row_hot,
    lane_hot,
    density,
    result,
    load_sem,
    out_sem,
    send_sem,
    recv_sem,
    tile_send,
    tile_recv,
):
    me = lax.axis_index("gx")
    planes, rows, lanes = pre.shape
    last = planes - 1
    chunk = rows // CHUNKS
    owned = noise_ref.shape[1]
    high = lax.rem(me + 1, count)
    low = lax.rem(me + count - 1, count)

    loads = [
        pltpu.make_async_copy(direction_hbm, states.at[0], load_sem.at[0]),
        pltpu.make_async_copy(kappa_hbm, kappa, load_sem.at[1]),
        pltpu.make_async_copy(velocity_hbm, velocity, load_sem.at[2]),
        pltpu.make_async_copy(prior_hbm, prior, load_sem.at[3]),
    ]
    for load in loads:
        load.start()

    barrier = pltpu.get_barrier_semaphore()

    def greet(offset, carry):
        pl.semaphore_signal(
            barrier,
            inc=1,
            device_id={"gx": lax.rem(me + offset, count)},
            device_id_type=pl.DeviceIdType.MESH,
        )
        return carry

    lax.fori_loop(1, count, greet, 0)

    tiles[me, 0:STEPS, :] = noise_ref[...]
    tiles[me, STEPS : STEPS + 1, :] = cell_ref[...].astype(jnp.float32)
    tiles[me, STEPS + 1 : STEPS + 2, :] = slab_ref[...].astype(jnp.float32)
    tiles[me, STEPS + 2 :, :] = jnp.zeros((tiles.shape[1] - STEPS - 2, owned), jnp.float32)

    @pl.when(me == 0)
    def _():
        halo_low[...] = jnp.zeros_like(halo_low)

    @pl.when(me == count - 1)
    def _():
        halo_high[...] = jnp.zeros_like(halo_high)

    def span(part):
        return pl.ds(part * chunk, chunk)

    def to_high(source, slot, part):
        return pltpu.make_async_remote_copy(
            src_ref=source.at[span(part)],
            dst_ref=halo_low.at[slot, span(part)],
            send_sem=send_sem.at[0, slot, part],
            recv_sem=recv_sem.at[0, slot, part],
            device_id={"gx": high},
            device_id_type=pl.DeviceIdType.MESH,
        )

    def to_low(source, slot, part):
        return pltpu.make_async_remote_copy(
            src_ref=source.at[span(part)],
            dst_ref=halo_high.at[slot, span(part)],
            send_sem=send_sem.at[1, slot, part],
            recv_sem=recv_sem.at[1, slot, part],
            device_id={"gx": low},
            device_id_type=pl.DeviceIdType.MESH,
        )

    started = []

    def send(top, bottom, slot, part):
        started.append((top, bottom, slot, part))

        @pl.when(me < count - 1)
        def _():
            to_high(top, slot, part).start()

        @pl.when(me > 0)
        def _():
            to_low(bottom, slot, part).start()

    def arrive(slot, part):
        @pl.when(me > 0)
        def _():
            to_high(states.at[0, 0], slot, part).wait_recv()

        @pl.when(me < count - 1)
        def _():
            to_low(states.at[0, 0], slot, part).wait_recv()

    pl.semaphore_wait(barrier, count - 1)
    loads[0].wait()
    for part in range(CHUNKS):
        send(states.at[0, last], states.at[0, 0], 0, part)

    def tile_copy(offset, source):
        return pltpu.make_async_remote_copy(
            src_ref=tiles.at[source],
            dst_ref=tiles.at[source],
            send_sem=tile_send.at[offset],
            recv_sem=tile_recv.at[offset],
            device_id={"gx": lax.rem(me + offset, count)},
            device_id_type=pl.DeviceIdType.MESH,
        )

    def tile_start(offset, carry):
        tile_copy(offset, me).start()
        return carry

    lax.fori_loop(1, count, tile_start, 0)

    row_at = lax.broadcasted_iota(jnp.int32, (rows, lanes), 0)
    lane_at = lax.broadcasted_iota(jnp.int32, (rows, lanes), 1)

    def next_row(value):
        return pltpu.roll(value, rows - 1, 0)

    def previous_row(value):
        return pltpu.roll(value, 1, 0)

    def next_lane(value):
        return pltpu.roll(value, lanes - 1, 1)

    def previous_lane(value):
        return pltpu.roll(value, 1, 1)

    loads[1].wait()
    loads[2].wait()
    for plane in range(planes):
        spread = kappa[plane]
        total = None
        edges = (None, None, row_at == rows - 1, row_at == 0, lane_at == lanes - 1, lane_at == 0)
        for column in range(3):
            speed = velocity[column, plane]
            for side in range(2):
                flow = jnp.maximum(-speed if side == 0 else speed, 0.0)
                piece = time_step * (spread + flow)
                total = piece if total is None else total + piece
                index = 2 * column + side
                edge = edges[index]
                coef[index, plane] = piece if edge is None else jnp.where(edge, 0.0, piece)
        centre[plane] = 1.0 - total

    def forward_local(step):
        for plane in range(planes):
            value = states[step, plane]
            result = centre[plane] * value
            if plane < last:
                result = result + coef[0, plane] * states[step, plane + 1]
            if plane > 0:
                result = result + coef[1, plane] * states[step, plane - 1]
            result = result + coef[2, plane] * next_row(value) + coef[3, plane] * previous_row(value)
            result = result + coef[4, plane] * next_lane(value) + coef[5, plane] * previous_lane(value)
            pre[plane] = result

    def prior_local(read, target, scale):
        for plane in range(planes):
            value = read(plane)
            result = (prior[plane] + 6.0) * value
            if plane < last:
                result = result - read(plane + 1)
            if plane > 0:
                result = result - read(plane - 1)
            result = result - jnp.where(row_at == rows - 1, 0.0, next_row(value))
            result = result - jnp.where(row_at == 0, 0.0, previous_row(value))
            result = result - jnp.where(lane_at == lanes - 1, 0.0, next_lane(value))
            result = result - jnp.where(lane_at == 0, 0.0, previous_lane(value))
            target[plane] = result

    prior_slot = 2 * STEPS
    cells_y = rows.bit_length() - 1

    def build_hot(first):
        def build(item, carry):
            tile = tiles.at[first + item]
            weight = tile[0:STEPS, :]
            cell = tile[STEPS : STEPS + 1, :].astype(jnp.int32)
            slab = tile[STEPS + 1 : STEPS + 2, :].astype(jnp.int32)
            row = jnp.where(slab == me, cell // lanes, -1)
            lane = cell % lanes
            at = pl.ds(pl.multiple_of(item * owned, owned), owned)
            tall = lax.broadcasted_iota(jnp.int32, (planes * rows, owned), 0)
            row_hot[:, at] = jnp.where(tall == row, 1.0, 0.0).astype(jnp.bfloat16)
            wide = lax.broadcasted_iota(jnp.int32, (lanes, owned), 0)
            here = wide == lane
            upper = weight.astype(jnp.bfloat16).astype(jnp.float32)
            lower = weight - upper
            for step in range(STEPS):
                lane_hot[step, 0:lanes, at] = jnp.where(here, upper[step : step + 1], 0.0).astype(jnp.bfloat16)
                lane_hot[step, lanes : 2 * lanes, at] = jnp.where(here, lower[step : step + 1], 0.0).astype(jnp.bfloat16)
            return carry

        lax.fori_loop(0, min(GROUP, count), build, 0)

    def add_density(step, first):
        both = lax.dot_general(
            row_hot[...],
            lane_hot[step],
            (((1,), (1,)), ((), ())),
            preferred_element_type=jnp.float32,
        )
        found = (both[:, :lanes] + both[:, lanes:]).reshape(planes, rows, lanes)
        if first:
            density[step] = found
        else:
            density[step] = density[step] + found

    def densities():
        build_hot(0)
        for step in range(STEPS):
            add_density(step, True)
        if count > GROUP:

            def more(block, carry):
                build_hot(block * GROUP)
                for step in range(STEPS):
                    add_density(step, False)
                return carry

            lax.fori_loop(1, count // GROUP, more, 0)

    for step in range(1, STEPS + 1):
        forward_local(step - 1)
        if step == 1:
            loads[3].wait()
            prior_local(lambda plane: states[0, plane], half, 1.0)
        if step == 2:
            half[0] = half[0] - halo_low[0]
            half[last] = half[last] - halo_high[0]
            for part in range(CHUNKS):
                send(half.at[last], half.at[0], prior_slot, part)
        if step == 3:

            def tile_wait(offset, carry):
                tile_copy(offset, me).wait_send()
                tile_copy(offset, lax.rem(me + count - offset, count)).wait_recv()
                return carry

            lax.fori_loop(1, count, tile_wait, 0)
            densities()
        if step == 4:
            prior_local(lambda plane: half[plane], smooth, 1.0)
        for part in range(CHUNKS):
            arrive(step - 1, part)
            at = span(part)
            for plane in range(planes):
                value = pre[plane, at]
                if plane == 0:
                    value = value + coef[1, 0, at] * halo_low[step - 1, at]
                if plane == last:
                    value = value + coef[0, last, at] * halo_high[step - 1, at]
                states[step, plane, at] = value
            if step < STEPS:
                send(states.at[step, last], states.at[step, 0], step, part)

    for order in range(STEPS):
        step = STEPS - order
        slot = STEPS + order
        for part in range(CHUNKS):
            at = span(part)
            if order > 0:
                arrive(slot - 1, part)
            for plane in range(planes):
                if order == 0:
                    value = density[step - 1, plane, at] * states[step, plane, at]
                else:
                    value = pre[plane, at]
                    if plane == 0:
                        value = value + halo_low[slot - 1, at]
                    if plane == last:
                        value = value + halo_high[slot - 1, at]
                result[plane, at] = value
                if plane == last:
                    sends[order, 0, at] = coef[0, last, at] * value
                if plane == 0:
                    sends[order, 1, at] = coef[1, 0, at] * value
            send(sends.at[order, 0], sends.at[order, 1], slot, part)
        for plane in range(planes):
            value = result[plane]
            total = centre[plane] * value
            if plane < last:
                total = total + coef[1, plane + 1] * result[plane + 1]
            if plane > 0:
                total = total + coef[0, plane - 1] * result[plane - 1]
            total = total + previous_row(coef[2, plane] * value) + next_row(coef[3, plane] * value)
            total = total + previous_lane(coef[4, plane] * value) + next_lane(coef[5, plane] * value)
            if step > 1:
                total = total + density[step - 2, plane] * states[step - 1, plane]
            else:
                total = total + prior_scale * smooth[plane]
            pre[plane] = total
        if order == 1:
            for part in range(CHUNKS):
                arrive(prior_slot, part)
            smooth[0] = smooth[0] - halo_low[prior_slot]
            smooth[last] = smooth[last] - halo_high[prior_slot]

    for part in range(CHUNKS):
        at = span(part)
        arrive(2 * STEPS - 1, part)
        for plane in range(planes):
            value = pre[plane, at]
            if plane == 0:
                value = value + halo_low[2 * STEPS - 1, at]
            if plane == last:
                value = value + halo_high[2 * STEPS - 1, at]
            result[plane, at] = value
    out = pltpu.make_async_copy(result, out_hbm, out_sem)
    out.start()

    @pl.when(me < count - 1)
    def _():
        for top, bottom, slot, part in started:
            to_high(top, slot, part).wait_send()

    @pl.when(me > 0)
    def _():
        for top, bottom, slot, part in started:
            to_low(bottom, slot, part).wait_send()

    out.wait()


def on_device(direction, kappa, velocity, prior_coef, noise_weight, sensor_cell, sensor_slab):
    count = lax.axis_size("gx")
    planes, rows, lanes = direction.shape
    owned = sensor_cell.shape[0]
    field = (planes, rows, lanes)
    slots = 2 * STEPS + 1
    group = min(GROUP, count) * owned
    hbm = pl.BlockSpec(memory_space=pl.ANY)
    vmem = pl.BlockSpec(memory_space=pltpu.VMEM)
    f32 = jnp.float32
    return pl.pallas_call(
        functools.partial(kernel, count),
        out_shape=jax.ShapeDtypeStruct(field, f32),
        in_specs=[hbm] * 4 + [vmem] * 3,
        out_specs=hbm,
        scratch_shapes=[
            pltpu.VMEM((STEPS + 1,) + field, f32),
            pltpu.VMEM(field, f32),
            pltpu.VMEM((3,) + field, f32),
            pltpu.VMEM(field, f32),
            pltpu.VMEM(field, f32),
            pltpu.VMEM((6,) + field, f32),
            pltpu.VMEM(field, f32),
            pltpu.VMEM(field, f32),
            pltpu.VMEM(field, f32),
            pltpu.VMEM((STEPS, 2, rows, lanes), f32),
            pltpu.VMEM((slots, rows, lanes), f32),
            pltpu.VMEM((slots, rows, lanes), f32),
            pltpu.VMEM((count, 8, owned), f32),
            pltpu.VMEM((planes * rows, group), jnp.bfloat16),
            pltpu.VMEM((STEPS, 2 * lanes, group), jnp.bfloat16),
            pltpu.VMEM((STEPS,) + field, f32),
            pltpu.VMEM(field, f32),
            pltpu.SemaphoreType.DMA((4,)),
            pltpu.SemaphoreType.DMA,
            pltpu.SemaphoreType.DMA((2, slots, CHUNKS)),
            pltpu.SemaphoreType.DMA((2, slots, CHUNKS)),
            pltpu.SemaphoreType.DMA((count,)),
            pltpu.SemaphoreType.DMA((count,)),
        ],
        compiler_params=pltpu.CompilerParams(
            collective_id=0, has_side_effects=True, vmem_limit_bytes=40 * 1024 * 1024
        ),
    )(
        direction,
        kappa,
        velocity,
        prior_coef,
        noise_weight,
        sensor_cell.reshape(1, owned),
        sensor_slab.reshape(1, owned),
    )


def solution(mesh):
    return jax.shard_map(
        on_device,
        mesh=mesh,
        in_specs=(
            P(("grp", "gx"), None, None),
            P(("grp", "gx"), None, None),
            P(None, ("grp", "gx"), None, None),
            P(("grp", "gx"), None, None),
            P(None, ("grp", "gx")),
            P(("grp", "gx")),
            P(("grp", "gx")),
        ),
        out_specs=P(("grp", "gx"), None, None),
        check_vma=False,
    )
```

time: 346 us -> 36.5 us (0.11)
  blocking collectives: 163 us -> 0 us
  other arithmetic: 59.4 us -> 0 us
  starting transfers between devices: 55.5 us -> 0 us
  local copies, waits for them, and re-layouts: 49.9 us -> 5.05 us
  Pallas kernels: 0 us -> 31.2 us
  waiting for transfers between devices: 16.1 us -> 0 us
    all_gather x6 -> x0, blocking collectives: 117 us -> none  [the longest x4 80 us: on_device(): add_misfit = lax.all_gather(weighted_rows[step], 'gx', axis=0, tiled=True)]
    scatter-add x4 -> x0, other arithmetic: 55.7 us -> none  [on_device(): adjoint_field.reshape(-1).at[target].add(jnp.where(valid, add_misfit, 0.0))]
    ppermute x20 -> x0, starting transfers between devices: 55.5 us -> none  [the longest x10 33.5 us: extended_2(): lax.ppermute(lax.slice_in_dim(block, block.shape[dim] - width, None, axis...]
    gather x4 -> x0, local copies, waits for them, and re-layouts: 47.1 us -> none  [record(): values = jnp.where(mine, jnp.take(state.reshape(-1), cells), 0.0)]
    unnamed x1 -> x0, blocking collectives: 45.4 us -> none
    pallas_call x0 -> x1, Pallas kernels: none -> 31.2 us  [on_device(): pl.pallas_call(functools.partial(kernel, count), out_shape=jax.ShapeDtype...]
    ppermute x20 -> x0, waiting for transfers between devices: 16.1 us -> none  [the longest x10 16 us: extended_2(): lax.ppermute(lax.slice_in_dim(block, 0, width, axis=dim), axis, backward)]
  transfers between devices with their start and end apart: 20 -> 0, of which waited for: 4 -> 0; matrix products, arithmetic and copies ran while one was open for 30% -> 0% of each run, Pallas kernels for 0% -> 0%
where the time goes in v1:
time: 36.5 us; the launch traced here: 36.3 us
  Pallas kernels  31.2 us (85%)
  local copies, waits for them, and re-layouts  5.05 us (14%)
    pallas_call x1, Pallas kernels, on_device(): pl.pallas_call(functools.partial(kernel, count), out_shape=jax.ShapeDtype...  31.2 us
    unnamed x15, local copies, waits for them, and re-layouts  5.05 us

profile of v1, /device:TPU:5, one launch (start us, length us, event | category | flops | bytes accessed | tf_op | source)
XLA Modules:
  0.0 36.3 jit_solution(2088641945918559270)
XLA Ops:
  0.0 0.0 copy-start.4
  0.0 0.0 copy-start.5
  0.0 0.0 copy-start.6
  0.0 0.7 %copy-done.4 = f32[4,128]{1,0:T(4,128)S(1)} copy-done((f32[4,128]{1,0:T(4,128)S(1)}, f32[4,128]{1,0:T(4,128)}, u32[]{:S(2)}) %copy-start.4) | copy-done | bytes 2072
  0.7 0.0 copy-done.5
  0.7 0.0 copy-done.6
  0.7 0.0 copy-start
  0.7 1.0 %copy-done = f32[3,2,128,128]{3,2,1,0:T(8,128)S(1)} copy-done((f32[3,2,128,128]{3,2,1,0:T(8,128)S(1)}, f32[3,2,128,128]{3,2,1,0:T(8,128)}, u32[]{:S(2)}) %copy-start) | copy-done | bytes 393240
  1.7 0.0 copy-start.1
  1.7 0.9 %copy-done.1 = f32[2,128,128]{2,1,0:T(8,128)S(1)} copy-done((f32[2,128,128]{2,1,0:T(8,128)S(1)}, f32[2,128,128]{2,1,0:T(8,128)}, u32[]{:S(2)}) %copy-start.1) | copy-done | bytes 131096
  2.6 0.0 copy-start.2
  2.6 0.9 %copy-done.2 = f32[2,128,128]{2,1,0:T(8,128)S(1)} copy-done((f32[2,128,128]{2,1,0:T(8,128)S(1)}, f32[2,128,128]{2,1,0:T(8,128)}, u32[]{:S(2)}) %copy-start.2) | copy-done | bytes 131096
  3.5 0.0 copy-start.3
  3.5 0.9 %copy-done.3 = f32[2,128,128]{2,1,0:T(8,128)S(1)} copy-done((f32[2,128,128]{2,1,0:T(8,128)S(1)}, f32[2,128,128]{2,1,0:T(8,128)}, u32[]{:S(2)}) %copy-start.3) | copy-done | bytes 131096
  4.4 31.2 %shard_map.73 = f32[2,128,128]{2,1,0:T(8,128)S(1)} custom-call(f32[2,128,128]{2,1,0:T(8,128)S(1)} %copy-done.1, f32[2,128,128]{2,1,0:T(8,128)S(1)} %copy-done.2, f32[3,2,128,128]{3,2,1,0:T(8,128)S(1)} %copy-done, f32[2,128,128]{2,1,0:T(8,128)S(1)} %copy-done.3, f32[4,128]{1,0:T(4,128)S(1)} %copy-done.4, s32[1,128]{1,0:T(1,128)S(1)} %bitcast.2, ...), custom_call_target="tpu_custom_call" | custom-call | tf_op jit(solution)/shard_map/pallas_call | solution.py:383
  35.6 0.7 %copy.9 = f32[2,128,128]{2,1,0:T(8,128)} copy(f32[2,128,128]{2,1,0:T(8,128)S(1)} %shard_map.73) | data formatting | bytes 262144
Async XLA Ops:
  0.0 0.7 %copy-start.4 = (f32[4,128]{1,0:T(4,128)S(1)}, f32[4,128]{1,0:T(4,128)}, u32[]{:S(2)}) copy-start(f32[4,128]{1,0:T(4,128)} %noise_ref.1) | copy-start | bytes 6148
  0.0 0.7 %copy-start.5 = (s32[128]{0:T(128)S(1)}, s32[128]{0:T(128)}, u32[]{:S(2)}) copy-start(s32[128]{0:T(128)} %param.12) | copy-start | bytes 1540
  0.0 0.7 %copy-start.6 = (s32[128]{0:T(128)S(1)}, s32[128]{0:T(128)}, u32[]{:S(2)}) copy-start(s32[128]{0:T(128)} %param.13) | copy-start | bytes 1540
  0.7 1.0 %copy-start = (f32[3,2,128,128]{3,2,1,0:T(8,128)S(1)}, f32[3,2,128,128]{3,2,1,0:T(8,128)}, u32[]{:S(2)}) copy-start(f32[3,2,128,128]{3,2,1,0:T(8,128)} %velocity_hbm.1) | copy-start | bytes 1179652
  1.7 0.9 %copy-start.1 = (f32[2,128,128]{2,1,0:T(8,128)S(1)}, f32[2,128,128]{2,1,0:T(8,128)}, u32[]{:S(2)}) copy-start(f32[2,128,128]{2,1,0:T(8,128)} %direction_hbm.1) | copy-start | bytes 393220
  2.6 0.9 %copy-start.2 = (f32[2,128,128]{2,1,0:T(8,128)S(1)}, f32[2,128,128]{2,1,0:T(8,128)}, u32[]{:S(2)}) copy-start(f32[2,128,128]{2,1,0:T(8,128)} %kappa_hbm.1) | copy-start | bytes 393220
  3.5 0.9 %copy-start.3 = (f32[2,128,128]{2,1,0:T(8,128)S(1)}, f32[2,128,128]{2,1,0:T(8,128)}, u32[]{:S(2)}) copy-start(f32[2,128,128]{2,1,0:T(8,128)} %prior_hbm.1) | copy-start | bytes 393220

commit v2 on v1

--- a/solution.py
+++ b/solution.py
@@ -21,9 +21,9 @@
     kappa_hbm,
     velocity_hbm,
     prior_hbm,
-    noise_ref,
-    cell_ref,
-    slab_ref,
+    noise_hbm,
+    cell_hbm,
+    slab_hbm,
     out_hbm,
     states,
     kappa,
@@ -42,6 +42,9 @@
     lane_hot,
     density,
     result,
+    noise_ref,
+    cell_ref,
+    slab_ref,
     load_sem,
     out_sem,
     send_sem,
@@ -58,6 +61,9 @@
     low = lax.rem(me + count - 1, count)
 
     loads = [
+        pltpu.make_async_copy(noise_hbm, noise_ref, load_sem.at[4]),
+        pltpu.make_async_copy(cell_hbm, cell_ref, load_sem.at[5]),
+        pltpu.make_async_copy(slab_hbm, slab_ref, load_sem.at[6]),
         pltpu.make_async_copy(direction_hbm, states.at[0], load_sem.at[0]),
         pltpu.make_async_copy(kappa_hbm, kappa, load_sem.at[1]),
         pltpu.make_async_copy(velocity_hbm, velocity, load_sem.at[2]),
@@ -79,6 +85,8 @@
 
     lax.fori_loop(1, count, greet, 0)
 
+    for load in loads[:3]:
+        load.wait()
     tiles[me, 0:STEPS, :] = noise_ref[...]
     tiles[me, STEPS : STEPS + 1, :] = cell_ref[...].astype(jnp.float32)
     tiles[me, STEPS + 1 : STEPS + 2, :] = slab_ref[...].astype(jnp.float32)
@@ -138,7 +146,7 @@
             to_low(states.at[0, 0], slot, part).wait_recv()
 
     pl.semaphore_wait(barrier, count - 1)
-    loads[0].wait()
+    loads[3].wait()
     for part in range(CHUNKS):
         send(states.at[0, last], states.at[0, 0], 0, part)
 
@@ -173,8 +181,8 @@
     def previous_lane(value):
         return pltpu.roll(value, 1, 1)
 
-    loads[1].wait()
-    loads[2].wait()
+    loads[4].wait()
+    loads[5].wait()
     for plane in range(planes):
         spread = kappa[plane]
         total = None
@@ -271,7 +279,7 @@
     for step in range(1, STEPS + 1):
         forward_local(step - 1)
         if step == 1:
-            loads[3].wait()
+            loads[6].wait()
             prior_local(lambda plane: states[0, plane], half, 1.0)
         if step == 2:
             half[0] = half[0] - halo_low[0]
@@ -377,13 +385,13 @@
     field = (planes, rows, lanes)
     slots = 2 * STEPS + 1
     group = min(GROUP, count) * owned
-    hbm = pl.BlockSpec(memory_space=pl.ANY)
+    hbm = pl.BlockSpec(memory_space=pltpu.HBM)
     vmem = pl.BlockSpec(memory_space=pltpu.VMEM)
     f32 = jnp.float32
     return pl.pallas_call(
         functools.partial(kernel, count),
         out_shape=jax.ShapeDtypeStruct(field, f32),
-        in_specs=[hbm] * 4 + [vmem] * 3,
+        in_specs=[hbm] * 7,
         out_specs=hbm,
         scratch_shapes=[
             pltpu.VMEM((STEPS + 1,) + field, f32),
@@ -403,7 +411,10 @@
             pltpu.VMEM((STEPS, 2 * lanes, group), jnp.bfloat16),
             pltpu.VMEM((STEPS,) + field, f32),
             pltpu.VMEM(field, f32),
-            pltpu.SemaphoreType.DMA((4,)),
+            pltpu.VMEM((STEPS, owned), f32),
+            pltpu.VMEM((1, owned), jnp.int32),
+            pltpu.VMEM((1, owned), jnp.int32),
+            pltpu.SemaphoreType.DMA((7,)),
             pltpu.SemaphoreType.DMA,
             pltpu.SemaphoreType.DMA((2, slots, CHUNKS)),
             pltpu.SemaphoreType.DMA((2, slots, CHUNKS)),
@@ -411,7 +422,7 @@
             pltpu.SemaphoreType.DMA((count,)),
         ],
         compiler_params=pltpu.CompilerParams(
-            collective_id=0, has_side_effects=True, vmem_limit_bytes=40 * 1024 * 1024
+            collective_id=0, has_side_effects=True, vmem_limit_bytes=63 * 1024 * 1024
         ),
     )(
         direction,

time: 36.5 us -> 32.7 us (0.90)
  local copies, waits for them, and re-layouts: 5.05 us -> 1.57 us
    unnamed x15 -> x1, local copies, waits for them, and re-layouts: 5.05 us -> 1.57 us
where the time goes in v2:
time: 32.7 us; the launch traced here: 32.5 us
  Pallas kernels  31 us (95%)
  local copies, waits for them, and re-layouts  1.57 us (5%)
    pallas_call x1, Pallas kernels, on_device(): pl.pallas_call(functools.partial(kernel, count), out_shape=jax.ShapeDtype...  31 us
    unnamed x1, local copies, waits for them, and re-layouts  1.57 us

profile of v2, /device:TPU:5, one launch (start us, length us, event | category | flops | bytes accessed | tf_op | source)
XLA Modules:
  0.0 32.5 jit_solution(14238771409252786826)
XLA Ops:
  0.0 31.0 %shard_map.73 = f32[2,128,128]{2,1,0:T(8,128)} custom-call(f32[2,128,128]{2,1,0:T(8,128)} %direction_hbm.1, f32[2,128,128]{2,1,0:T(8,128)} %kappa_hbm.1, f32[3,2,128,128]{3,2,1,0:T(8,128)} %velocity_hbm.1, f32[2,128,128]{2,1,0:T(8,128)} %prior_hbm.1, f32[4,128]{1,0:T(4,128)} %noise_hbm.1, s32[1,128]{1,0:T(1,128)} %bitcast.2, s32[1,128]{1,0:T(1,128)} %bitcast.3), custom_call_target="tpu_custom_call" | custom-call | tf_op jit(solution)/shard_map/pallas_call | solution.py:391
  31.0 1.6 %copy.9 = f32[2,128,128]{2,1,0:T(8,128)} copy(f32[2,128,128]{2,1,0:T(8,128)} %shard_map.73) | data formatting | bytes 262144

commit v3 on v2

--- a/solution.py
+++ b/solution.py
@@ -10,6 +10,7 @@
 STEPS = 4
 CHUNKS = 2
 GROUP = 16
+RADIX = 4
 
 time_step = 0.25
 prior_scale = 0.01
@@ -74,16 +75,30 @@
 
     barrier = pltpu.get_barrier_semaphore()
 
-    def greet(offset, carry):
+    def greet(target):
         pl.semaphore_signal(
-            barrier,
-            inc=1,
-            device_id={"gx": lax.rem(me + offset, count)},
-            device_id_type=pl.DeviceIdType.MESH,
+            barrier, inc=1, device_id={"gx": target}, device_id_type=pl.DeviceIdType.MESH
         )
-        return carry
-
-    lax.fori_loop(1, count, greet, 0)
+
+    @pl.when(me > 0)
+    def _():
+        greet(low)
+
+    @pl.when(me < count - 1)
+    def _():
+        greet(high)
+
+    rounds = gather_rounds(count)
+
+    def member(stride, radix, offset):
+        digit = lax.rem(me // stride, radix)
+        return me + (lax.rem(digit + offset, radix) - digit) * stride
+
+    greeted = jnp.where((me == 0) | (me == count - 1), 1, 2)
+    for stride, radix in rounds:
+        for offset in range(1, radix):
+            greet(member(stride, radix, offset))
+        greeted = greeted + radix - 1
 
     for load in loads[:3]:
         load.wait()
@@ -145,26 +160,34 @@
         def _():
             to_low(states.at[0, 0], slot, part).wait_recv()
 
-    pl.semaphore_wait(barrier, count - 1)
+    pl.semaphore_wait(barrier, greeted)
     loads[3].wait()
     for part in range(CHUNKS):
         send(states.at[0, last], states.at[0, 0], 0, part)
 
-    def tile_copy(offset, source):
+    def tile_copy(turn, offset, source):
+        stride, radix = rounds[turn]
+        block = tiles.at[pl.ds((source // stride) * stride, stride)]
         return pltpu.make_async_remote_copy(
-            src_ref=tiles.at[source],
-            dst_ref=tiles.at[source],
-            send_sem=tile_send.at[offset],
-            recv_sem=tile_recv.at[offset],
-            device_id={"gx": lax.rem(me + offset, count)},
+            src_ref=block,
+            dst_ref=block,
+            send_sem=tile_send.at[turn, offset],
+            recv_sem=tile_recv.at[turn, offset],
+            device_id={"gx": member(stride, radix, offset)},
             device_id_type=pl.DeviceIdType.MESH,
         )
 
-    def tile_start(offset, carry):
-        tile_copy(offset, me).start()
-        return carry
-
-    lax.fori_loop(1, count, tile_start, 0)
+    def tile_start(turn):
+        for offset in range(1, rounds[turn][1]):
+            tile_copy(turn, offset, me).start()
+
+    def tile_finish(turn):
+        stride, radix = rounds[turn]
+        for offset in range(1, radix):
+            tile_copy(turn, offset, me).wait_send()
+            tile_copy(turn, offset, member(stride, radix, radix - offset)).wait_recv()
+
+    tile_start(0)
 
     row_at = lax.broadcasted_iota(jnp.int32, (rows, lanes), 0)
     lane_at = lax.broadcasted_iota(jnp.int32, (rows, lanes), 1)
@@ -225,7 +248,6 @@
             target[plane] = result
 
     prior_slot = 2 * STEPS
-    cells_y = rows.bit_length() - 1
 
     def build_hot(first):
         def build(item, carry):
@@ -286,15 +308,21 @@
             half[last] = half[last] - halo_high[0]
             for part in range(CHUNKS):
                 send(half.at[last], half.at[0], prior_slot, part)
+        if step == 2:
+            tile_finish(0)
+            if len(rounds) > 1:
+                tile_start(1)
         if step == 3:
-
-            def tile_wait(offset, carry):
-                tile_copy(offset, me).wait_send()
-                tile_copy(offset, lax.rem(me + count - offset, count)).wait_recv()
-                return carry
-
-            lax.fori_loop(1, count, tile_wait, 0)
-            densities()
+            for turn in range(1, len(rounds)):
+                tile_finish(turn)
+                if turn + 1 < len(rounds):
+                    tile_start(turn + 1)
+            if count > GROUP:
+                densities()
+            else:
+                build_hot(0)
+        if step == 4 and count <= GROUP:
+            add_density(STEPS - 1, True)
         if step == 4:
             prior_local(lambda plane: half[plane], smooth, 1.0)
         for part in range(CHUNKS):
@@ -332,6 +360,8 @@
                 if plane == 0:
                     sends[order, 1, at] = coef[1, 0, at] * value
             send(sends.at[order, 0], sends.at[order, 1], slot, part)
+        if step > 1 and count <= GROUP:
+            add_density(step - 2, True)
         for plane in range(planes):
             value = result[plane]
             total = centre[plane] * value
@@ -378,6 +408,16 @@
     out.wait()
 
 
+def gather_rounds(count):
+    rounds = []
+    stride = 1
+    while stride < count:
+        radix = min(RADIX, count // stride)
+        rounds.append((stride, radix))
+        stride *= radix
+    return rounds
+
+
 def on_device(direction, kappa, velocity, prior_coef, noise_weight, sensor_cell, sensor_slab):
     count = lax.axis_size("gx")
     planes, rows, lanes = direction.shape
@@ -418,8 +458,8 @@
             pltpu.SemaphoreType.DMA,
             pltpu.SemaphoreType.DMA((2, slots, CHUNKS)),
             pltpu.SemaphoreType.DMA((2, slots, CHUNKS)),
-            pltpu.SemaphoreType.DMA((count,)),
-            pltpu.SemaphoreType.DMA((count,)),
+            pltpu.SemaphoreType.DMA((len(gather_rounds(count)), RADIX)),
+            pltpu.SemaphoreType.DMA((len(gather_rounds(count)), RADIX)),
         ],
         compiler_params=pltpu.CompilerParams(
             collective_id=0, has_side_effects=True, vmem_limit_bytes=63 * 1024 * 1024

time: 32.7 us -> 31.6 us (0.966)
  Pallas kernels: 31 us -> 29.9 us
    pallas_call x1, Pallas kernels: 31 us -> 29.9 us  [on_device(): pl.pallas_call(functools.partial(kernel, count), out_shape=jax.ShapeDtype...]
where the time goes in v3:
time: 31.6 us; the launch traced here: 31.5 us
  Pallas kernels  29.9 us (95%)
  local copies, waits for them, and re-layouts  1.57 us (5%)
    pallas_call x1, Pallas kernels, on_device(): pl.pallas_call(functools.partial(kernel, count), out_shape=jax.ShapeDtype...  29.9 us
    unnamed x1, local copies, waits for them, and re-layouts  1.57 us

profile of v3, /device:TPU:5, one launch (start us, length us, event | category | flops | bytes accessed | tf_op | source)
XLA Modules:
  0.0 31.5 jit_solution(4655413356590642704)
XLA Ops:
  0.0 29.9 %shard_map.73 = f32[2,128,128]{2,1,0:T(8,128)} custom-call(f32[2,128,128]{2,1,0:T(8,128)} %direction_hbm.1, f32[2,128,128]{2,1,0:T(8,128)} %kappa_hbm.1, f32[3,2,128,128]{3,2,1,0:T(8,128)} %velocity_hbm.1, f32[2,128,128]{2,1,0:T(8,128)} %prior_hbm.1, f32[4,128]{1,0:T(4,128)} %noise_hbm.1, s32[1,128]{1,0:T(1,128)} %bitcast.2, s32[1,128]{1,0:T(1,128)} %bitcast.3), custom_call_target="tpu_custom_call" | custom-call | tf_op jit(solution)/shard_map/pallas_call | solution.py:431
  29.9 1.6 %copy.9 = f32[2,128,128]{2,1,0:T(8,128)} copy(f32[2,128,128]{2,1,0:T(8,128)} %shard_map.73) | data formatting | bytes 262144

commit v4 on v3

--- a/solution.py
+++ b/solution.py
@@ -8,7 +8,7 @@
 from jax.sharding import PartitionSpec as P
 
 STEPS = 4
-CHUNKS = 2
+CHUNKS = 4
 GROUP = 16
 RADIX = 4
 
@@ -160,6 +160,23 @@
         def _():
             to_low(states.at[0, 0], slot, part).wait_recv()
 
+    def settle(upper, arrived, finish, source, slot, part):
+        copy = to_high if upper else to_low
+        back = to_low if upper else to_high
+        inside = me < count - 1 if upper else me > 0
+
+        @pl.when(inside)
+        def _():
+            if arrived is not None:
+                back(states.at[0, 0], arrived, part).wait_recv()
+            finish(True)
+            if source is not None:
+                copy(source, slot, part).start()
+
+        @pl.when(jnp.logical_not(inside))
+        def _():
+            finish(False)
+
     pl.semaphore_wait(barrier, greeted)
     loads[3].wait()
     for part in range(CHUNKS):
@@ -326,40 +343,49 @@
         if step == 4:
             prior_local(lambda plane: half[plane], smooth, 1.0)
         for part in range(CHUNKS):
-            arrive(step - 1, part)
             at = span(part)
-            for plane in range(planes):
-                value = pre[plane, at]
-                if plane == 0:
-                    value = value + coef[1, 0, at] * halo_low[step - 1, at]
-                if plane == last:
-                    value = value + coef[0, last, at] * halo_high[step - 1, at]
-                states[step, plane, at] = value
             if step < STEPS:
-                send(states.at[step, last], states.at[step, 0], step, part)
+                started.append((states.at[step, last], states.at[step, 0], step, part))
+            for plane in range(1, last):
+                states[step, plane, at] = pre[plane, at]
+            for upper in (True, False):
+                plane = last if upper else 0
+
+                def finish(near, plane=plane, upper=upper, at=at, step=step):
+                    value = pre[plane, at]
+                    if near:
+                        halo = halo_high if upper else halo_low
+                        side = 0 if upper else 1
+                        value = value + coef[side, plane, at] * halo[step - 1, at]
+                    states[step, plane, at] = value
+
+                source = states.at[step, plane] if step < STEPS else None
+                settle(upper, step - 1, finish, source, step, part)
 
     for order in range(STEPS):
         step = STEPS - order
         slot = STEPS + order
+        if order == 0:
+            pre[...] = density[step - 1] * states[step]
         for part in range(CHUNKS):
             at = span(part)
-            if order > 0:
-                arrive(slot - 1, part)
-            for plane in range(planes):
-                if order == 0:
-                    value = density[step - 1, plane, at] * states[step, plane, at]
-                else:
+            started.append((sends.at[order, 0], sends.at[order, 1], slot, part))
+            for plane in range(1, last):
+                result[plane, at] = pre[plane, at]
+            for upper in (True, False):
+                plane = last if upper else 0
+
+                def finish(near, plane=plane, upper=upper, at=at, step=step, order=order, slot=slot):
                     value = pre[plane, at]
-                    if plane == 0:
-                        value = value + halo_low[slot - 1, at]
-                    if plane == last:
-                        value = value + halo_high[slot - 1, at]
-                result[plane, at] = value
-                if plane == last:
-                    sends[order, 0, at] = coef[0, last, at] * value
-                if plane == 0:
-                    sends[order, 1, at] = coef[1, 0, at] * value
-            send(sends.at[order, 0], sends.at[order, 1], slot, part)
+                    if near and order > 0:
+                        halo = halo_high if upper else halo_low
+                        value = value + halo[slot - 1, at]
+                    result[plane, at] = value
+                    side = 0 if upper else 1
+                    sends[order, side, at] = coef[side, plane, at] * value
+
+                arrived = slot - 1 if order > 0 else None
+                settle(upper, arrived, finish, sends.at[order, 0 if upper else 1], slot, part)
         if step > 1 and count <= GROUP:
             add_density(step - 2, True)
         for plane in range(planes):
@@ -382,6 +408,7 @@
             smooth[0] = smooth[0] - halo_low[prior_slot]
             smooth[last] = smooth[last] - halo_high[prior_slot]
 
+    outs = []
     for part in range(CHUNKS):
         at = span(part)
         arrive(2 * STEPS - 1, part)
@@ -392,8 +419,8 @@
             if plane == last:
                 value = value + halo_high[2 * STEPS - 1, at]
             result[plane, at] = value
-    out = pltpu.make_async_copy(result, out_hbm, out_sem)
-    out.start()
+        outs.append(pltpu.make_async_copy(result.at[:, at], out_hbm.at[:, at], out_sem.at[part]))
+        outs[-1].start()
 
     @pl.when(me < count - 1)
     def _():
@@ -405,7 +432,8 @@
         for top, bottom, slot, part in started:
             to_low(bottom, slot, part).wait_send()
 
-    out.wait()
+    for out in outs:
+        out.wait()
 
 
 def gather_rounds(count):
@@ -455,7 +483,7 @@
             pltpu.VMEM((1, owned), jnp.int32),
             pltpu.VMEM((1, owned), jnp.int32),
             pltpu.SemaphoreType.DMA((7,)),
-            pltpu.SemaphoreType.DMA,
+            pltpu.SemaphoreType.DMA((CHUNKS,)),
             pltpu.SemaphoreType.DMA((2, slots, CHUNKS)),
             pltpu.SemaphoreType.DMA((2, slots, CHUNKS)),
             pltpu.SemaphoreType.DMA((len(gather_rounds(count)), RADIX)),

time: 31.6 us -> 31.5 us (level)
  no operation moved by 1% of the time
where the time goes in v4:
time: 31.5 us; the launch traced here: 31.3 us
  Pallas kernels  29.7 us (94%)
  local copies, waits for them, and re-layouts  1.57 us (5%)
    pallas_call x1, Pallas kernels, on_device(): pl.pallas_call(functools.partial(kernel, count), out_shape=jax.ShapeDtype...  29.7 us
    unnamed x1, local copies, waits for them, and re-layouts  1.57 us

profile of v4, /device:TPU:5, one launch (start us, length us, event | category | flops | bytes accessed | tf_op | source)
XLA Modules:
  0.0 31.3 jit_solution(16665170552686984427)
XLA Ops:
  0.0 29.7 %shard_map.73 = f32[2,128,128]{2,1,0:T(8,128)} custom-call(f32[2,128,128]{2,1,0:T(8,128)} %direction_hbm.1, f32[2,128,128]{2,1,0:T(8,128)} %kappa_hbm.1, f32[3,2,128,128]{3,2,1,0:T(8,128)} %velocity_hbm.1, f32[2,128,128]{2,1,0:T(8,128)} %prior_hbm.1, f32[4,128]{1,0:T(4,128)} %noise_hbm.1, s32[1,128]{1,0:T(1,128)} %bitcast.2, s32[1,128]{1,0:T(1,128)} %bitcast.3), custom_call_target="tpu_custom_call" | custom-call | tf_op jit(solution)/shard_map/pallas_call | solution.py:459
  29.8 1.6 %copy.9 = f32[2,128,128]{2,1,0:T(8,128)} copy(f32[2,128,128]{2,1,0:T(8,128)} %shard_map.73) | data formatting | bytes 262144

commit v5 on v4

--- a/solution.py
+++ b/solution.py
@@ -70,7 +70,7 @@
         pltpu.make_async_copy(velocity_hbm, velocity, load_sem.at[2]),
         pltpu.make_async_copy(prior_hbm, prior, load_sem.at[3]),
     ]
-    for load in loads:
+    for load in loads[3:4] + loads[:3] + loads[4:]:
         load.start()
 
     barrier = pltpu.get_barrier_semaphore()

time: 31.5 us -> 31.5 us (level)
  no operation moved by 1% of the time
where the time goes in v5:
time: 31.5 us; the launch traced here: 31.3 us
  Pallas kernels  29.7 us (94%)
  local copies, waits for them, and re-layouts  1.57 us (5%)
    pallas_call x1, Pallas kernels, on_device(): pl.pallas_call(functools.partial(kernel, count), out_shape=jax.ShapeDtype...  29.7 us
    unnamed x1, local copies, waits for them, and re-layouts  1.57 us

profile of v5, /device:TPU:5, one launch (start us, length us, event | category | flops | bytes accessed | tf_op | source)
XLA Modules:
  0.0 31.3 jit_solution(6941767707055768387)
XLA Ops:
  0.0 29.7 %shard_map.73 = f32[2,128,128]{2,1,0:T(8,128)} custom-call(f32[2,128,128]{2,1,0:T(8,128)} %direction_hbm.1, f32[2,128,128]{2,1,0:T(8,128)} %kappa_hbm.1, f32[3,2,128,128]{3,2,1,0:T(8,128)} %velocity_hbm.1, f32[2,128,128]{2,1,0:T(8,128)} %prior_hbm.1, f32[4,128]{1,0:T(4,128)} %noise_hbm.1, s32[1,128]{1,0:T(1,128)} %bitcast.2, s32[1,128]{1,0:T(1,128)} %bitcast.3), custom_call_target="tpu_custom_call" | custom-call | tf_op jit(solution)/shard_map/pallas_call | solution.py:459
  29.8 1.6 %copy.9 = f32[2,128,128]{2,1,0:T(8,128)} copy(f32[2,128,128]{2,1,0:T(8,128)} %shard_map.73) | data formatting | bytes 262144
